TPU v7x, 512 devices: a whole 4x4x16 slice. The times are simulated.
512 devices in a mesh: row: 16 (over z), col: 32 (over x, y, core).
Axes of the slice: x: 4, y: 4, z: 16, core: 2. Of those that a mesh axis runs over, the one named last changes fastest.
Arguments:
- matrix_slab: float32 [6, 4096, 8192], P(None, 'row', 'col'), may hold values from 0 to 3, as said below
Outputs:
- factored: float32 [6, 4096, 8192], P(None, 'row', 'col')
Inputs may be any that keep to these rules, and one draw needn't show every extreme that they name: `matrix_slab`: the first 8192 columns of a symmetric positive definite matrix: a sum of two Matern covariances of points in the plane plus a positive diagonal.
All inputs are finite; a program needn't handle non-finite values.
Results may differ from a plain program's by a relative error of at most 0.0003.
Values sent between devices are 32-bit elements; how exact they have to be, the bound alone decides.
A program may use at most 64 MiB of HBM per device.

v0:
```python
import jax
import jax.numpy as jnp
from jax import lax
from jax.sharding import PartitionSpec as P


def from_root(block, axis, holder):
    block = jnp.where(lax.axis_index(axis) == holder, block, jnp.zeros_like(block))
    return lax.psum(block, axis)


def lower_products(panel_rows, partner):
    return jnp.einsum("mab,cb->mac", panel_rows, partner, precision=lax.Precision.HIGHEST)


def home_block(panel_rows, home_group):
    return lax.dynamic_index_in_dim(panel_rows, home_group, 0, keepdims=False)


def factor_panel(work, step, grid_col, global_rows):
    size = work.shape[1]
    identity = jnp.eye(size, dtype=work.dtype)
    diag_block = from_root(work[0], "row", step)
    lower_diag = jnp.linalg.cholesky(jnp.where(grid_col == step, diag_block, identity))
    flat = work.reshape(-1, size)
    solved = jax.scipy.linalg.solve_triangular(lower_diag, flat.T, lower=True).T
    solved = solved.reshape(work.shape)
    rows = global_rows[:, None, None]
    return jnp.where(
        rows > step, solved, jnp.where(rows == step, lower_diag[None], jnp.zeros_like(solved))
    )


def on_device(matrix_slab):
    row_count = lax.axis_size("row")
    grid_row = lax.axis_index("row")
    grid_col = lax.axis_index("col")
    groups = matrix_slab.shape[0]
    global_rows = jnp.arange(groups, dtype=jnp.int32) * row_count + grid_row
    home_group = grid_col // row_count
    home_row = grid_col % row_count
    work = matrix_slab
    for step in range(2):
        panel = factor_panel(work, step, grid_col, global_rows)
        row_panel = from_root(panel, "col", step)
        partner = from_root(home_block(row_panel, home_group), "row", home_row)
        updated = work - lower_products(row_panel, partner)
        work = jnp.where(grid_col > step, updated, jnp.where(grid_col == step, panel, work))
    keep = (global_rows >= grid_col)[:, None, None]
    return jnp.where(keep, work, jnp.zeros_like(work))


def solution(mesh):
    in_specs = (P(None, "row", "col"),)
    out_specs = P(None, "row", "col")
    return jax.shard_map(
        on_device, mesh=mesh, in_specs=in_specs, out_specs=out_specs, check_vma=False
    )
```

profile of v0, /device:TPU:4, one launch (start us, length us, event | category | flops | bytes accessed | tf_op | source)
XLA Modules:
  0.0 993.7 jit_solution(1305191332402818069)
XLA Ops:
  6.5 1.9 copy.23
  8.4 0.8 fusion.7
  9.3 0.5 iota_multiply_fusion
  9.8 139.8 %all-reduce.8.cloned.1.call-done = f32[256,256]{0,1:T(8,128)} async-done(((f32[256,256]{0,1:T(8,128)}), f32[256,256]{0,1:T(8,128)}) %all-reduce.8.cloned.1.call-update) | async-done | bytes 262160 | tf_op jit(solution)/shard_map/psum | solution.py:9
  149.7 0.1 copy.17
  149.9 0.7 copy-done.4
  150.6 11.7 %cholesky.130 = f32[128,128]{1,0:T(8,128)S(1)} custom-call(f32[128,128]{1,0:T(8,128)S(1)} %cholesky.194), custom_call_target="Cholesky" | custom-call | tf_op jit(solution)/shard_map/jit(cholesky)/cholesky | solution.py:24
  162.3 9.8 custom-call.13
  172.2 1.0 constant_dynamic-update-slice_fusion.3
  173.2 1.1 convolution_subtract_fusion.3
  174.3 11.7 %cholesky.147 = f32[128,128]{1,0:T(8,128)S(1)} custom-call(f32[128,128]{1,0:T(8,128)S(1)} %convolution_subtract_fusion.3), custom_call_target="Cholesky" | custom-call | tf_op jit(solution)/shard_map/jit(cholesky)/cholesky | solution.py:24
  186.1 0.7 compare_reduce_fusion.2
  188.1 0.7 fusion.14
  188.8 0.7 triangular_solve.75
  189.5 4.5 while.4
  190.0 0.7 fusion.40
  190.6 1.3 bitcast_dynamic-update-slice_fusion.4
  192.0 0.7 fusion.40
  192.7 1.3 bitcast_dynamic-update-slice_fusion.4
  194.0 19.7 %custom-call.14 = f32[2,128,128]{1,2,0:T(8,128)S(1)} custom-call(f32[2,128,128]{2,1,0:T(8,128)S(1)} %get-tuple-element.21), custom_call_target="InvertDiagBlocksLowerTriangular" | custom-call | tf_op jit(solution)/shard_map/jit(_solve_triangular)/triangular_solve | solution.py:26
  213.7 0.9 fusion.4
  214.6 1.4 convolution_subtract_fusion.1
  216.0 0.9 fusion.20
  217.0 1.6 copy.18
  218.6 1.9 copy.20
  220.7 1.4 fusion
  222.2 133.2 %all-reduce.10.cloned.1.call-done = f32[6,256,256]{1,2,0:T(8,128)} async-done(((f32[6,256,256]{1,2,0:T(8,128)}), f32[6,256,256]{1,2,0:T(8,128)}) %all-reduce.10.cloned.1.call-update) | async-done | bytes 1572880 | tf_op jit(solution)/shard_map/psum | solution.py:9
  355.5 1.7 select_bitcast_fusion.1
  357.2 136.5 %all-reduce.12.cloned.1.call-done = f32[256,256]{0,1:T(8,128)} async-done(((f32[256,256]{0,1:T(8,128)}), f32[256,256]{0,1:T(8,128)}) %all-reduce.12.cloned.1.call-update) | async-done | bytes 262160 | tf_op jit(solution)/shard_map/psum | solution.py:9
  493.7 3.7 select_select_fusion.2
  497.5 0.7 fusion.6
  498.2 0.2 all-reduce.16.cloned.1.call-start
  498.5 0.5 copy.27
  498.9 131.8 %all-reduce.14.cloned.1.call-done = f32[256,256]{0,1:T(8,128)} async-done(((f32[256,256]{0,1:T(8,128)}), f32[256,256]{0,1:T(8,128)}) %all-reduce.14.cloned.1.call-update) | async-done | bytes 262160 | tf_op jit(solution)/shard_map/psum | solution.py:9
  630.7 0.8 copy.26
  631.6 1.0 fusion.9
  632.6 0.7 copy-done.5
  633.3 11.7 %cholesky.164 = f32[128,128]{1,0:T(8,128)S(1)} custom-call(f32[128,128]{1,0:T(8,128)S(1)} %cholesky.197), custom_call_target="Cholesky" | custom-call | tf_op jit(solution)/shard_map/jit(cholesky)/cholesky | solution.py:24
  645.0 9.8 custom-call.15
  654.9 1.0 constant_dynamic-update-slice_fusion.1
  655.9 1.1 convolution_subtract_fusion.2
  657.0 11.7 %cholesky.181 = f32[128,128]{1,0:T(8,128)S(1)} custom-call(f32[128,128]{1,0:T(8,128)S(1)} %convolution_subtract_fusion.2), custom_call_target="Cholesky" | custom-call | tf_op jit(solution)/shard_map/jit(cholesky)/cholesky | solution.py:24
  668.8 0.6 compare_reduce_fusion
  669.4 0.7 compare_reduce_fusion.1
  671.4 1.7 fusion.12
  673.1 4.2 while.5
  673.3 0.6 fusion.41
  673.9 1.4 bitcast_dynamic-update-slice_fusion.5
  675.3 0.6 fusion.41
  675.9 1.4 bitcast_dynamic-update-slice_fusion.5
  677.3 0.6 copy-done.6
  677.9 20.5 %custom-call.16 = f32[2,128,128]{1,2,0:T(8,128)S(1)} custom-call(f32[2,128,128]{2,1,0:T(8,128)} %copy-done.6), custom_call_target="InvertDiagBlocksLowerTriangular" | custom-call | tf_op jit(solution)/shard_map/jit(_solve_triangular)/triangular_solve | solution.py:26
  698.4 0.9 fusion.2
  699.3 1.4 convolution_subtract_fusion
  700.7 0.9 fusion.16
  701.7 1.6 copy.28
  703.3 1.9 copy.30
  705.2 1.1 copy.29
  706.3 1.4 fusion.1
  707.7 133.3 %all-reduce.16.cloned.1.call-done = f32[6,256,256]{1,2,0:T(8,128)} async-done(((f32[6,256,256]{1,2,0:T(8,128)}), f32[6,256,256]{1,2,0:T(8,128)}) %all-reduce.16.cloned.1.call-update) | async-done | bytes 1572880 | tf_op jit(solution)/shard_map/psum | solution.py:9
  841.0 1.7 select_bitcast_fusion
  842.7 136.5 %all-reduce.18.cloned.1.call-done = f32[256,256]{0,1:T(8,128)} async-done(((f32[256,256]{0,1:T(8,128)}), f32[256,256]{0,1:T(8,128)}) %all-reduce.18.cloned.1.call-update) | async-done | bytes 262160 | tf_op jit(solution)/shard_map/psum | solution.py:9
  979.2 4.4 select_select_fusion
  983.6 3.0 copy.34
  (45 shorter events, 1.0 us)
Async XLA Ops:
  6.5 143.1 %all-reduce.8.cloned.1.call-start = ((), (), s32[]{:S(2)}) async-start(), calls=%async_computation | async-start | bytes 524288 | tf_op jit(solution)/shard_map/psum | solution.py:9
  8.4 163.8 %copy-start = (f32[6,256,256]{1,2,0:T(8,128)}, f32[6,256,256]{1,2,0:T(8,128)S(1)}, u32[]{:S(2)}) copy-start(f32[6,256,256]{1,2,0:T(8,128)S(1)} %copy.23) | copy-start | bytes 4718596
  9.3 346.2 %all-reduce.10.cloned.1.call-start = ((), (), s32[]{:S(2)}) async-start(), calls=%async_computation.1 | async-start | bytes 3145728 | tf_op jit(solution)/shard_map/psum | solution.py:9
  149.9 0.7 copy-start.4
  150.6 63.1 %copy-start.1 = (f32[6,256,256]{2,1,0:T(8,128)S(1)}, f32[6,256,256]{2,1,0:T(8,128)}, u32[]{:S(2)}) copy-start(f32[6,256,256]{2,1,0:T(8,128)} %param.4) | copy-start | bytes 4718596
  218.6 1.9 copy-start.3
  222.1 271.6 %all-reduce.12.cloned.1.call-start = ((), (), s32[]{:S(2)}) async-start(), calls=%async_computation.2 | async-start | bytes 524288 | tf_op jit(solution)/shard_map/psum | solution.py:9
  357.2 273.5 %all-reduce.14.cloned.1.call-start = ((), (), s32[]{:S(2)}) async-start(), calls=%async_computation.3 | async-start | bytes 524288 | tf_op jit(solution)/shard_map/psum | solution.py:9
  498.2 342.8 %all-reduce.16.cloned.1.call-start = ((), (), s32[]{:S(2)}) async-start(), calls=%async_computation.4 | async-start | bytes 3145728 | tf_op jit(solution)/shard_map/psum | solution.py:9
  632.6 0.7 copy-start.5
  668.8 2.6 copy-start.2
  677.3 0.7 copy-start.6
  707.7 271.6 %all-reduce.18.cloned.1.call-start = ((), (), s32[]{:S(2)}) async-start(), calls=%async_computation.5 | async-start | bytes 524288 | tf_op jit(solution)/shard_map/psum | solution.py:9
Sparse Core Ops, SparseCore 0:
  9.7 139.9 all-reduce.7
  222.2 133.1 all-reduce.9
  357.8 135.9 all-reduce.11
  498.3 132.3 all-reduce.13
  707.8 133.1 all-reduce.15
  843.3 135.9 all-reduce.17
where the time goes:
time: 1000 us; the launch traced here: 994 us
  waiting for transfers between devices  811 us (81%)
  other arithmetic  121 us (12%)
  local copies, waits for them, and re-layouts  25.3 us (3%)
  matrix products  18.7 us (2%)
  between operations  16.6 us (2%)
    psum x6, waiting for transfers between devices, from_root(): return lax.psum(block, axis)  811 us
    another operation x13, other arithmetic, factor_panel(): jnp.linalg.cholesky(jnp.where(grid_col == step, diag_block, identity))  68.7 us
    another operation x5, other arithmetic, factor_panel(): solved = jax.scipy.linalg.solve_triangular(lower_diag, flat.T, lower=True).T  43.1 us
  transfers between devices with their start and end apart: 6, of which 6 were waited for; matrix products, arithmetic and copies ran while one was open for 0% of the time, Pallas kernels for 0%

commit v1 on v0

v1 whole, which is shorter than its diff:
```python
import functools

import jax
import jax.numpy as jnp
from jax import lax
from jax.experimental import pallas as pl
from jax.experimental.pallas import tpu as pltpu
from jax.sharding import PartitionSpec as P

HI = lax.Precision.HIGHEST
SB = 128

def dot(a, b):
    return lax.dot_general(a, b, (((1,), (0,)), ((), ())), precision=HI, preferred_element_type=jnp.float32)

def dot_nt(a, b):
    return lax.dot_general(a, b, (((1,), (1,)), ((), ())), precision=HI, preferred_element_type=jnp.float32)

def dot_tn(a, b):
    return lax.dot_general(a, b, (((0,), (0,)), ((), ())), precision=HI, preferred_element_type=jnp.float32)

def lanes(col):
    return jnp.broadcast_to(col, (8, SB))

def eliminate(strips):
    sub = lax.broadcasted_iota(jnp.int32, (8, SB), 0)
    lane = lax.broadcasted_iota(jnp.int32, (8, SB), 1)
    strips = list(strips)
    scales = []
    for k in range(16):
        cur = strips[k]
        col = [lanes(cur[:, 8 * k + j:8 * k + j + 1]) for j in range(8)]
        scale = jnp.zeros((8, SB), jnp.float32)
        rows, inner = [], []
        for j in range(8):
            pivot = lanes(col[j][j:j + 1])
            inv = 1.0 / pivot
            scale = jnp.where(sub == j, lax.rsqrt(pivot), scale)
            row = jnp.where(lane == 8 * k + j, pivot + 1.0, lanes(cur[j:j + 1])) * inv
            below = jnp.where(sub > j, col[j], 0.0)
            part = []
            for i in range(j + 1, 8):
                ratio = lanes(col[i][j:j + 1]) * inv
                col[i] = col[i] - below * ratio
                part.append(ratio)
            cur = cur - below * row
            rows.append(row)
            inner.append(part)
        strips[k] = cur
        scales.append(scale)
        for t in range(k + 1, 16):
            acc = strips[t]
            c = [lanes(acc[:, 8 * k + j:8 * k + j + 1]) for j in range(8)]
            for j in range(8):
                for i in range(j + 1, 8):
                    c[i] = c[i] - c[j] * inner[j][i - j - 1]
                acc = acc - c[j] * rows[j]
            strips[t] = acc
    return strips, scales

def factor_block(aug, xs, s):
    off = pl.multiple_of(s * SB, SB)
    strips = [aug[pl.ds(off + 8 * t, 8), pl.ds(off, SB)] for t in range(16)]
    strips, scales = eliminate(strips)
    sub = lax.broadcasted_iota(jnp.int32, (8, SB), 0)
    lane = lax.broadcasted_iota(jnp.int32, (8, SB), 1)
    for t in range(16):
        q = sub + 8 * t
        xs[8 * t:8 * t + 8, :] = jnp.where(lane < q, strips[t] * scales[t], jnp.where(lane == q, scales[t], 0.0))

def factor(aug, xs, nsb, width):
    def step(s, carry):
        off = pl.multiple_of(s * SB, SB)
        factor_block(aug, xs, s)
        x = xs[...]
        y = dot(x, aug[pl.ds(off, SB), :])
        def trail(t, c):
            toff = pl.multiple_of(t * SB, SB)
            low = dot_nt(aug[pl.ds(toff, SB), pl.ds(off, SB)], x)
            aug[pl.ds(toff, SB), :] = aug[pl.ds(toff, SB), :] - dot(low, y)
            return c
        lax.fori_loop(s + 1, nsb, trail, 0)
        aug[pl.ds(off, SB), :] = y
        return carry
    lax.fori_loop(0, nsb, step, 0)


NB = 256
N_ROW = 16
N_COL = 32
CHUNKS = 12
ROWS = 32
MESH = pl.DeviceIdType.MESH
CORNER = ((0, 0), (1, 0), (1, 1))


def send(src, dst, send_sem, recv_sem, device):
    return pltpu.make_async_remote_copy(
        src_ref=src, dst_ref=dst, send_sem=send_sem, recv_sem=recv_sem, device_id=device, device_id_type=MESH
    )


def kernel(
    x_ref, o_ref, own, corner, top, panel, aug, xs,
    own_sem, local_sem, corner_send, corner_recv, top_send, top_recv, tree_send, tree_recv, pair_send, pair_recv,
):
    row = lax.axis_index("row")
    col = lax.axis_index("col")
    core = lax.rem(col, 2)
    y = lax.rem(col // 2, 4)
    x = col // 8
    is_root = col < 2

    own_copy = pltpu.make_async_copy(x_ref, own, own_sem)
    own_copy.start()
    barrier = pltpu.get_barrier_semaphore()

    def greet_col(c, carry):
        @pl.when(c != col)
        def _():
            pl.semaphore_signal(barrier, inc=1, device_id=(row, c), device_id_type=MESH)
        return carry

    def greet_row(r, carry):
        @pl.when(r != row)
        def _():
            pl.semaphore_signal(barrier, inc=1, device_id=(r, col), device_id_type=MESH)
        return carry

    lax.fori_loop(0, N_COL, greet_col, 0)
    lax.fori_loop(0, N_ROW, greet_row, 0)
    own_copy.wait()

    @pl.when(is_root)
    def _():
        c0 = pltpu.make_async_copy(own, panel.at[core], local_sem.at[0])
        c0.start()
        c0.wait()

    for b, (hr, hc) in enumerate(CORNER):
        @pl.when((row == hr) & (col == hc))
        def _():
            c1 = pltpu.make_async_copy(own.at[0], corner.at[b], local_sem.at[1])
            c1.start()
            c1.wait()

    @pl.when(row < 2)
    def _():
        c2 = pltpu.make_async_copy(own.at[0], top.at[row], local_sem.at[2])
        c2.start()
        c2.wait()

    pl.semaphore_wait(barrier, N_COL + N_ROW - 2)

    def strip(b, c):
        return corner.at[b, pl.ds(pl.multiple_of(c * 8, 8), 8), :]

    def strips(b, n):
        return corner.at[b, pl.ds(0, 8 * n), :]

    def each(n, me, body):
        def one(i, carry):
            @pl.when(i != me)
            def _():
                body(i)
            return carry
        lax.fori_loop(0, n, one, 0)

    for b, (hr, hc) in enumerate(CORNER):
        @pl.when((row == hr) & (col == hc))
        def _():
            each(N_COL, col, lambda c: send(
                strip(b, c), strip(b, c), corner_send.at[0, b], corner_recv.at[0, b], (row, c)).start())

    for b, (hr, hc) in enumerate(CORNER):
        mine = strip(b, col)

        @pl.when((row == hr) & (col != hc))
        def _():
            send(mine, mine, corner_send.at[0, b], corner_recv.at[0, b], (row, col)).wait_recv()

        @pl.when(row == hr)
        def _():
            each(N_ROW, row, lambda r: send(
                mine, mine, corner_send.at[1, b], corner_recv.at[1, b], (r, col)).start())

        @pl.when(row != hr)
        def _():
            send(mine, mine, corner_send.at[1, b], corner_recv.at[1, b], (row, col)).wait_recv()

        def spread(c):
            @pl.when((row != hr) | (c != hc))
            def _():
                send(mine, mine, corner_send.at[2, b], corner_recv.at[2, b], (row, c)).start()
        each(N_COL, col, spread)

    def rounds(t, carry):
        for q in range(2):
            delta = lax.rem(row - q + N_ROW, N_ROW)
            depth = jnp.where(delta <= 8, delta, N_ROW - delta)
            m = t - depth
            piece = top.at[q, pl.ds(pl.multiple_of(jnp.clip(m, 0, 3) * 64, 64), 64), :]
            slot = jnp.clip(m, 0, 3)

            @pl.when((m >= 0) & (m < 4))
            def _():
                @pl.when(delta > 0)
                def _():
                    send(piece, piece, top_send.at[q, 0], top_recv.at[q, slot], (row, col)).wait_recv()

                @pl.when(delta < 8)
                def _():
                    send(piece, piece, top_send.at[q, 0], top_recv.at[q, slot],
                         (lax.rem(row + 1, N_ROW), col)).start()

                @pl.when((delta == 0) | (delta >= 10))
                def _():
                    send(piece, piece, top_send.at[q, 1], top_recv.at[q, slot],
                         (lax.rem(row + N_ROW - 1, N_ROW), col)).start()

        for tree in range(4):
            u, v, step_u, step_v = (
                (x, y, (1, 0), (0, 1)),
                (y, lax.rem(4 - x, 4), (0, 1), (3, 0)),
                (lax.rem(4 - x, 4), lax.rem(4 - y, 4), (3, 0), (0, 3)),
                (lax.rem(4 - y, 4), x, (0, 3), (1, 0)),
            )[tree]
            depth = jnp.where(v == 0, u, jnp.where(u >= 1, u + v, v + 4))
            m = t - depth
            slot = jnp.clip(m, 0, CHUNKS - 1)
            piece = panel.at[core, slot // 2, pl.ds(pl.multiple_of(64 * tree + 32 * lax.rem(slot, 2), 32), ROWS), :]

            def at(step):
                return (row, lax.rem(x + step[0], 4) * 8 + lax.rem(y + step[1], 4) * 2 + core)

            @pl.when((m >= 0) & (m < CHUNKS))
            def _():
                @pl.when((u != 0) | (v != 0))
                def _():
                    send(piece, piece, tree_send.at[tree, 0], tree_recv.at[tree, slot], (row, col)).wait_recv()

                @pl.when(((v == 0) & (u <= 2)) | ((v >= 1) & (u == 3)))
                def _():
                    send(piece, piece, tree_send.at[tree, 0], tree_recv.at[tree, slot], at(step_u)).start()

                @pl.when((u >= 1) & (v <= 2))
                def _():
                    send(piece, piece, tree_send.at[tree, 1], tree_recv.at[tree, slot], at(step_v)).start()

                send(piece, piece, pair_send, pair_recv, (row, col + 1 - 2 * core)).start()
        return carry

    lax.fori_loop(0, CHUNKS + 7, rounds, 0)

    for b, (hr, hc) in enumerate(CORNER):
        @pl.when((row != hr) | (col != hc))
        def _():
            send(strips(b, 31), strips(b, 31), corner_send.at[2, b], corner_recv.at[2, b], (row, col)).wait_recv()
    send(panel.at[1 - core], panel.at[1 - core], pair_send, pair_recv, (row, col)).wait_recv()

    aug[0:256, 0:256] = corner[0]
    aug[256:512, 0:256] = corner[1]
    aug[0:256, 256:512] = corner[1].T
    aug[256:512, 256:512] = corner[2]
    aug[0:256, 512:768] = top[0]
    aug[256:512, 512:768] = top[1]
    wide_r = lax.broadcasted_iota(jnp.int32, (512, 512), 0)
    wide_c = lax.broadcasted_iota(jnp.int32, (512, 512), 1)
    aug[:, 768:1280] = jnp.where(wide_r == wide_c, 1.0, 0.0)
    factor(aug, xs, 4, 1280)
    tall_r = lax.broadcasted_iota(jnp.int32, (512, 256), 0)
    tall_c = lax.broadcasted_iota(jnp.int32, (512, 256), 1)
    pick = jnp.where(tall_r == tall_c + NB * col, -1.0, 0.0)
    rhs = jnp.where(is_root, pick, aug[:, 512:768])
    aug[:, 512:768] = dot_tn(aug[:, 768:1280], rhs)

    sq_r = lax.broadcasted_iota(jnp.int32, (NB, NB), 0)
    sq_c = lax.broadcasted_iota(jnp.int32, (NB, NB), 1)

    def update(g, carry):
        index = g * N_ROW + row
        change = dot(panel[0, g], aug[0:256, 512:768]) + dot(panel[1, g], aug[256:512, 512:768])
        value = jnp.where(is_root, 0.0, own[g]) - change
        keep = (index > col) | ((index == col) & ((sq_r >= sq_c) | jnp.logical_not(is_root)))
        o_ref[g] = jnp.where(keep, value, 0.0)
        return carry

    lax.fori_loop(0, 6, update, 0)

    for b, (hr, hc) in enumerate(CORNER):
        @pl.when((row == hr) & (col == hc))
        def _():
            send(strips(b, 31), strips(b, 31), corner_send.at[0, b], corner_recv.at[0, b], (row, col)).wait_send()

        @pl.when(row == hr)
        def _():
            send(strips(b, 15), strips(b, 15), corner_send.at[1, b], corner_recv.at[1, b], (row, col)).wait_send()

        @pl.when((row == hr) & (col != hc))
        def _():
            send(strips(b, 30), strips(b, 30), corner_send.at[2, b], corner_recv.at[2, b], (row, col)).wait_send()

        @pl.when((row != hr) | (col == hc))
        def _():
            send(strips(b, 31), strips(b, 31), corner_send.at[2, b], corner_recv.at[2, b], (row, col)).wait_send()

    for q in range(2):
        delta = lax.rem(row - q + N_ROW, N_ROW)
        whole = top.at[q]

        @pl.when(delta < 8)
        def _():
            send(whole, whole, top_send.at[q, 0], top_recv.at[q, 0], (row, col)).wait_send()

        @pl.when((delta == 0) | (delta >= 10))
        def _():
            send(whole, whole, top_send.at[q, 1], top_recv.at[q, 0], (row, col)).wait_send()

    for tree in range(4):
        u, v = (
            (x, y), (y, lax.rem(4 - x, 4)), (lax.rem(4 - x, 4), lax.rem(4 - y, 4)), (lax.rem(4 - y, 4), x),
        )[tree]
        part = panel.at[core, :, pl.ds(64 * tree, 64), :]

        @pl.when(((v == 0) & (u <= 2)) | ((v >= 1) & (u == 3)))
        def _():
            send(part, part, tree_send.at[tree, 0], tree_recv.at[tree, 0], (row, col)).wait_send()

        @pl.when((u >= 1) & (v <= 2))
        def _():
            send(part, part, tree_send.at[tree, 1], tree_recv.at[tree, 0], (row, col)).wait_send()
    send(panel.at[core], panel.at[core], pair_send, pair_recv, (row, col)).wait_send()


def on_device(slab):
    return pl.pallas_call(
        kernel,
        out_shape=jax.ShapeDtypeStruct(slab.shape, jnp.float32),
        in_specs=[pl.BlockSpec(memory_space=pl.ANY)],
        out_specs=pl.BlockSpec(memory_space=pltpu.VMEM),
        scratch_shapes=[
            pltpu.VMEM((6, NB, NB), jnp.float32),
            pltpu.VMEM((3, NB, NB), jnp.float32),
            pltpu.VMEM((2, NB, NB), jnp.float32),
            pltpu.VMEM((2, 6, NB, NB), jnp.float32),
            pltpu.VMEM((512, 1280), jnp.float32),
            pltpu.VMEM((SB, SB), jnp.float32),
            pltpu.SemaphoreType.DMA,
            pltpu.SemaphoreType.DMA((3,)),
            pltpu.SemaphoreType.DMA((3, 3)),
            pltpu.SemaphoreType.DMA((3, 3)),
            pltpu.SemaphoreType.DMA((2, 2)),
            pltpu.SemaphoreType.DMA((2, 4)),
            pltpu.SemaphoreType.DMA((4, 2)),
            pltpu.SemaphoreType.DMA((4, CHUNKS)),
            pltpu.SemaphoreType.DMA,
            pltpu.SemaphoreType.DMA,
        ],
        compiler_params=pltpu.CompilerParams(
            collective_id=0, has_side_effects=True, vmem_limit_bytes=48 * 2**20
        ),
    )(slab)


def solution(mesh):
    spec = P(None, "row", "col")
    return jax.shard_map(on_device, mesh=mesh, in_specs=(spec,), out_specs=spec, check_vma=False)
```

time: 1000 us -> 117 us (0.12)
  the two profiles are of different devices: /device:TPU:4 before, /device:TPU:169 now
where the time goes in v1:
time: 117 us
  Pallas kernels  115 us (98%)
  local copies, waits for them, and re-layouts  2.55 us (2%)
    pallas_call x1, Pallas kernels, on_device(): pl.pallas_call(kernel, out_shape=jax.ShapeDtypeStruct(slab.shape, jnp.flo...  115 us
    unnamed x3, local copies, waits for them, and re-layouts  2.55 us

profile of v1, /device:TPU:169, one launch (start us, length us, event | category | flops | bytes accessed | tf_op | source)
XLA Modules:
  0.0 117.1 jit_solution(6421246319395441415)
XLA Ops:
  0.0 0.0 copy-start
  0.0 1.4 %copy-done = f32[6,256,256]{2,1,0:T(8,128)S(1)} copy-done((f32[6,256,256]{2,1,0:T(8,128)S(1)}, f32[6,256,256]{2,1,0:T(8,128)}, u32[]{:S(2)}) %copy-start) | copy-done | bytes 1572888
  1.4 114.6 %shard_map.17 = f32[6,256,256]{2,1,0:T(8,128)S(1)} custom-call(f32[6,256,256]{2,1,0:T(8,128)S(1)} %copy-done), custom_call_target="tpu_custom_call" | custom-call | tf_op jit(solution)/shard_map/pallas_call | solution.py:336
  116.0 1.1 copy.3
Async XLA Ops:
  0.0 1.4 %copy-start = (f32[6,256,256]{2,1,0:T(8,128)S(1)}, f32[6,256,256]{2,1,0:T(8,128)}, u32[]{:S(2)}) copy-start(f32[6,256,256]{2,1,0:T(8,128)} %x_ref.1) | copy-start | bytes 4718596

commit v2 on v0

v2 whole, which is shorter than its diff:
```python
import jax
import jax.numpy as jnp
from jax import lax
from jax.experimental import pallas as pl
from jax.experimental.pallas import tpu as pltpu
from jax.sharding import PartitionSpec as P

HI = lax.Precision.HIGHEST
SB = 128

def dot(a, b):
    return lax.dot_general(a, b, (((1,), (0,)), ((), ())), precision=HI, preferred_element_type=jnp.float32)

def dot_nt(a, b):
    return lax.dot_general(a, b, (((1,), (1,)), ((), ())), precision=HI, preferred_element_type=jnp.float32)

def dot_tn(a, b):
    return lax.dot_general(a, b, (((0,), (0,)), ((), ())), precision=HI, preferred_element_type=jnp.float32)

def lanes(col):
    return jnp.broadcast_to(col, (8, SB))

def eliminate(strips, after):
    sub = lax.broadcasted_iota(jnp.int32, (8, SB), 0)
    lane = lax.broadcasted_iota(jnp.int32, (8, SB), 1)
    strips = list(strips)
    scales = []
    for k in range(16):
        cur = strips[k]
        col = [lanes(cur[:, 8 * k + j:8 * k + j + 1]) for j in range(8)]
        scale = jnp.zeros((8, SB), jnp.float32)
        rows, inner = [], []
        for j in range(8):
            pivot = lanes(col[j][j:j + 1])
            inv = 1.0 / pivot
            scale = jnp.where(sub == j, lax.rsqrt(pivot), scale)
            row = jnp.where(lane == 8 * k + j, pivot + 1.0, lanes(cur[j:j + 1])) * inv
            below = jnp.where(sub > j, col[j], 0.0)
            part = []
            for i in range(j + 1, 8):
                ratio = lanes(col[i][j:j + 1]) * inv
                col[i] = col[i] - below * ratio
                part.append(ratio)
            cur = cur - below * row
            rows.append(row)
            inner.append(part)
        strips[k] = cur
        scales.append(scale)
        for t in range(k + 1, 16):
            acc = strips[t]
            c = [lanes(acc[:, 8 * k + j:8 * k + j + 1]) for j in range(8)]
            for j in range(8):
                for i in range(j + 1, 8):
                    c[i] = c[i] - c[j] * inner[j][i - j - 1]
                acc = acc - c[j] * rows[j]
            strips[t] = acc
        after(k)
    return strips, scales


NB = 256
N_ROW = 16
N_COL = 32
MESH = pl.DeviceIdType.MESH
TREE_PARTS = 12
TOP_PARTS = 8
SKEW = 3
EARLY = 3


def send(src, dst, send_sem, recv_sem, device):
    return pltpu.make_async_remote_copy(
        src_ref=src, dst_ref=dst, send_sem=send_sem, recv_sem=recv_sem, device_id=device, device_id_type=MESH
    )


def kernel(
    x_ref, o_ref, own, first, low, high, top, panel, aug, xs,
    own_sem, scatter_send, scatter_recv, ring_send, ring_recv, plane_send, plane_recv, twin_send, twin_recv,
    top_send, top_recv, tree_send, tree_recv, pair_send, pair_recv,
):
    row = lax.axis_index("row")
    col = lax.axis_index("col")
    core = lax.rem(col, 2)
    chip = col // 2
    x = chip // 4
    y = lax.rem(chip, 4)
    is_root = col < 2
    twin = (row, col + 1 - 2 * core)
    here = (row, col)

    own_copy = pltpu.make_async_copy(x_ref, own, own_sem)
    own_copy.start()

    def loop(n, body):
        def one(i, carry):
            body(i)
            return carry
        lax.fori_loop(0, n, one, 0)

    def plane_peer(j):
        o = 10 + j
        o = jnp.where(o >= 16, o - 15, o)
        return lax.rem(x + o // 4, 4) * 4 + lax.rem(y + lax.rem(o, 4), 4)

    def ring_peer(j):
        half = (j + 1) // 2
        return lax.rem(row + 8 + jnp.where(lax.rem(j, 2) == 1, -half, half) + N_ROW, N_ROW)

    barrier = pltpu.get_barrier_semaphore()
    loop(15, lambda j: pl.semaphore_signal(barrier, inc=1, device_id=(ring_peer(j), col), device_id_type=MESH))
    loop(15, lambda j: pl.semaphore_signal(
        barrier, inc=1, device_id=(row, plane_peer(j) * 2 + core), device_id_type=MESH))
    pl.semaphore_signal(barrier, inc=1, device_id=twin, device_id_type=MESH)
    own_copy.wait()

    def first_piece(i):
        return first.at[pl.ds(pl.multiple_of(i * 8, 8), 8), :]

    holds_00 = (row == 0) & (col == 0)
    holds_10 = (row == 1) & (col == 0)
    holds_11 = (row == 1) & (col == 1)

    @pl.when(holds_00)
    def _():
        first[0:8, :] = own[0, 0:8, 0:SB]
        low[0, 0:8, :] = own[0, SB:SB + 8, :]

    @pl.when(holds_10)
    def _():
        low[0, 8:24, :] = own[0, 0:16, :]

    @pl.when(holds_11)
    def _():
        high[0] = own[0, 0:16, :]

    @pl.when(is_root)
    def _():
        panel[core] = own[...]

    @pl.when(row < 2)
    def _():
        top[row] = own[0]

    pl.semaphore_wait(barrier, 31)

    def own_rows(start, n):
        return own.at[0, pl.ds(pl.multiple_of(start, 8), n), :]

    @pl.when(holds_00)
    def _():
        loop(15, lambda j: send(
            own.at[0, pl.ds(pl.multiple_of(plane_peer(j) * 8, 8), 8), pl.ds(0, SB)], first_piece(plane_peer(j)),
            scatter_send.at[0], scatter_recv.at[0], (row, plane_peer(j) * 2)).start())
        loop(15, lambda j: send(
            own_rows(SB + plane_peer(j) * 8, 8), low.at[plane_peer(j), pl.ds(0, 8), :],
            scatter_send.at[1], scatter_recv.at[1], (row, plane_peer(j) * 2)).start())

    @pl.when(holds_10)
    def _():
        loop(15, lambda j: send(
            own_rows(plane_peer(j) * 16, 16), low.at[plane_peer(j), pl.ds(8, 16), :],
            scatter_send.at[2], scatter_recv.at[2], (row, plane_peer(j) * 2)).start())

    @pl.when(holds_11)
    def _():
        loop(15, lambda j: send(
            own_rows(plane_peer(j) * 16, 16), high.at[plane_peer(j)],
            scatter_send.at[3], scatter_recv.at[3], (row, plane_peer(j) * 2 + 1)).start())

    pieces = (
        (first_piece(chip), 0, 0),
        (low.at[chip, pl.ds(0, 8), :], 0, 0),
        (low.at[chip, pl.ds(8, 16), :], 1, 0),
        (high.at[chip], 1, 1),
    )
    for n, (piece, start, carrier) in enumerate(pieces):
        @pl.when((row == start) & (core == carrier))
        def _():
            @pl.when(chip != 0)
            def _():
                send(piece, piece, scatter_send.at[n], scatter_recv.at[n], here).wait_recv()
            loop(15, lambda j: send(
                piece, piece, ring_send.at[n], ring_recv.at[n], (ring_peer(j), col)).start())

    def ring_arrived(n):
        piece, start, _ = pieces[n]

        @pl.when(row != start)
        def _():
            send(piece, piece, ring_send.at[n], ring_recv.at[n], here).wait_recv()

    @pl.when(core == 0)
    def _():
        ring_arrived(0)
        loop(15, lambda j: send(
            first_piece(chip), first_piece(chip), plane_send.at[0], plane_recv.at[0],
            (row, plane_peer(j) * 2)).start())
        ring_arrived(1)
        ring_arrived(2)
        loop(15, lambda j: send(
            low.at[chip], low.at[chip], plane_send.at[1], plane_recv.at[1], (row, plane_peer(j) * 2)).start())

    @pl.when(core == 1)
    def _():
        ring_arrived(3)
        loop(15, lambda j: send(
            high.at[chip], high.at[chip], plane_send.at[2], plane_recv.at[2],
            (row, plane_peer(j) * 2 + 1)).start())

    q = lax.rem(row, 2)
    delta = row - q
    top_depth = jnp.where(delta <= 8, delta, N_ROW - delta) // 2

    def top_to(offset):
        return (lax.rem(row + offset + N_ROW, N_ROW), col)

    def top_step(t):
        m = t - SKEW * top_depth
        slot = jnp.clip(m, 0, TOP_PARTS - 1)
        piece = top.at[q, pl.ds(pl.multiple_of(slot * 32, 32), 32), :]

        def go(kind, offset):
            send(piece, piece, top_send.at[kind], top_recv.at[q, slot], top_to(offset)).start()

        @pl.when((m >= 0) & (m < TOP_PARTS))
        def _():
            @pl.when(delta > 0)
            def _():
                send(piece, piece, top_send.at[0], top_recv.at[q, slot], here).wait_recv()

            @pl.when(delta < 8)
            def _():
                go(0, 2)

            @pl.when((delta == 0) | (delta >= 12))
            def _():
                go(1, -2)

            @pl.when((delta >= 2) & (delta <= 8))
            def _():
                go(2, -1)

            @pl.when(delta >= 8)
            def _():
                go(3, 1)

    def hops(p):
        return jnp.where(p == 0, 0, jnp.where(p == 2, 2, 1))

    def tree_step(t):
        for h in range(2):
            u, v = (x, y) if h == 0 else (y, x)
            p = jnp.where(v == 0, u, v)

            def at(u2, v2):
                x2, y2 = (u2, v2) if h == 0 else (v2, u2)
                return (row, x2 * 8 + y2 * 2 + core)

            m = t - SKEW * (hops(u) + hops(v))
            slot = jnp.clip(m, 0, TREE_PARTS - 1)
            start = 128 * h + 64 * lax.rem(slot, 2)
            part = panel.at[core, slot // 2, pl.ds(pl.multiple_of(start, 64), 64), :]
            half0 = panel.at[core, slot // 2, pl.ds(pl.multiple_of(start, 32), 32), :]
            half1 = panel.at[core, slot // 2, pl.ds(pl.multiple_of(start + 32, 32), 32), :]

            def go(piece, kind, half, device):
                send(piece, piece, tree_send.at[h, kind], tree_recv.at[h, slot, half], device).start()

            @pl.when((m >= 0) & (m < TREE_PARTS))
            def _():
                @pl.when((p == 1) | (p == 3))
                def _():
                    send(part, part, tree_send.at[h, 0], tree_recv.at[h, slot, 0], here).wait_recv()

                @pl.when(p == 2)
                def _():
                    send(half0, half0, tree_send.at[h, 0], tree_recv.at[h, slot, 0], here).wait_recv()
                    send(half1, half1, tree_send.at[h, 0], tree_recv.at[h, slot, 1], here).wait_recv()

                @pl.when((v == 0) & (u == 0))
                def _():
                    go(part, 0, 0, at(1, 0))
                    go(part, 1, 0, at(3, 0))

                @pl.when(p == 1)
                def _():
                    go(half0, 2, 0, at(jnp.where(v == 0, 2, u), jnp.where(v == 0, 0, 2)))

                @pl.when(p == 3)
                def _():
                    go(half1, 2, 1, at(jnp.where(v == 0, 2, u), jnp.where(v == 0, 0, 2)))

                @pl.when(v == 0)
                def _():
                    go(part, 3, 0, at(u, 1))
                    go(part, 4, 0, at(u, 3))

                send(part, part, pair_send.at[h], pair_recv.at[h], twin).start()

    def tick(t):
        top_step(t)
        tree_step(t)

    for t in range(EARLY):
        tick(jnp.int32(t))

    @pl.when(core == 0)
    def _():
        send(first.at[pl.ds(0, 120), :], first.at[pl.ds(0, 120), :], plane_send.at[0], plane_recv.at[0], here).wait_recv()
        send(first, first, twin_send.at[0], twin_recv.at[0], twin).start()

    @pl.when(core == 1)
    def _():
        send(first, first, twin_send.at[0], twin_recv.at[0], here).wait_recv()

    def rest_in_plane():
        @pl.when(core == 0)
        def _():
            send(low.at[pl.ds(0, 15)], low.at[pl.ds(0, 15)], plane_send.at[1], plane_recv.at[1], here).wait_recv()
            send(low, low, twin_send.at[1], twin_recv.at[1], twin).start()

        @pl.when(core == 1)
        def _():
            send(high.at[pl.ds(0, 15)], high.at[pl.ds(0, 15)], plane_send.at[2], plane_recv.at[2], here).wait_recv()
            send(high, high, twin_send.at[2], twin_recv.at[2], twin).start()

    def rest_from_twin():
        @pl.when(core == 1)
        def _():
            send(low, low, twin_send.at[1], twin_recv.at[1], here).wait_recv()

        @pl.when(core == 0)
        def _():
            send(high, high, twin_send.at[2], twin_recv.at[2], here).wait_recv()

        for i in range(16):
            aug[SB + 8 * i:SB + 8 * i + 8, 0:NB] = low[i, 0:8, :]
            aug[NB + 16 * i:NB + 16 * i + 16, 0:NB] = low[i, 8:24, :]
            aug[NB + 16 * i:NB + 16 * i + 16, NB:2 * NB] = high[i]
        aug[0:SB, SB:NB] = aug[SB:NB, 0:SB].T
        aug[0:NB, NB:2 * NB] = aug[NB:2 * NB, 0:NB].T

    wide_r = lax.broadcasted_iota(jnp.int32, (512, 512), 0)
    wide_c = lax.broadcasted_iota(jnp.int32, (512, 512), 1)
    aug[:, 512:1024] = jnp.where(wide_r == wide_c, 1.0, 0.0)
    aug[0:SB, 0:SB] = first[...]
    sub = lax.broadcasted_iota(jnp.int32, (8, SB), 0)
    lane = lax.broadcasted_iota(jnp.int32, (8, SB), 1)

    def factor_step(s, carry):
        off = pl.multiple_of(s * SB, SB)

        def after(k):
            if k % 3 == 2:
                if k == 8:
                    pl.when(s == 0)(rest_in_plane)
                tick(EARLY + 6 * s + k // 3)

        strips, scales = eliminate([aug[pl.ds(off + 8 * t, 8), pl.ds(off, SB)] for t in range(16)], after)
        for t in range(16):
            diag = sub + 8 * t
            xs[8 * t:8 * t + 8, :] = jnp.where(
                lane < diag, strips[t] * scales[t], jnp.where(lane == diag, scales[t], 0.0))
        pl.when(s == 0)(rest_from_twin)
        inverse = xs[...]
        done = dot(inverse, aug[pl.ds(off, SB), :])

        def trail(t, c):
            toff = pl.multiple_of(t * SB, SB)
            lower = dot_nt(aug[pl.ds(toff, SB), pl.ds(off, SB)], inverse)
            aug[pl.ds(toff, SB), :] = aug[pl.ds(toff, SB), :] - dot(lower, done)
            return c
        lax.fori_loop(s + 1, 4, trail, 0)
        aug[pl.ds(off, SB), :] = done
        tick(EARLY + 6 * s + 5)
        return carry

    lax.fori_loop(0, 4, factor_step, 0)

    def top_arrived(m):
        piece = top.at[1 - q, pl.ds(pl.multiple_of(m * 32, 32), 32), :]
        send(piece, piece, top_send.at[0], top_recv.at[1 - q, m], here).wait_recv()

    @pl.when((row != 0) | (q != 1))
    def _():
        loop(TOP_PARTS, top_arrived)

    tall_r = lax.broadcasted_iota(jnp.int32, (512, NB), 0)
    tall_c = lax.broadcasted_iota(jnp.int32, (512, NB), 1)
    solved = dot(aug[:, 512:768], top[0]) + dot(aug[:, 768:1024], top[1])
    aug[:, 0:NB] = jnp.where(is_root, jnp.where(tall_r == tall_c + NB * col, -1.0, 0.0), solved)
    aug[:, NB:2 * NB] = dot_tn(aug[:, 512:1024], aug[:, 0:NB])

    for h in range(2):
        part = panel.at[1 - core, :, pl.ds(128 * h, 128), :]
        send(part, part, pair_send.at[h], pair_recv.at[h], here).wait_recv()

    sq_r = lax.broadcasted_iota(jnp.int32, (NB, NB), 0)
    sq_c = lax.broadcasted_iota(jnp.int32, (NB, NB), 1)

    def update(g):
        index = g * N_ROW + row
        change = dot(panel[0, g], aug[0:NB, NB:2 * NB]) + dot(panel[1, g], aug[NB:2 * NB, NB:2 * NB])
        value = jnp.where(is_root, 0.0, own[g]) - change
        keep = (index > col) | ((index == col) & ((sq_r >= sq_c) | jnp.logical_not(is_root)))
        o_ref[g] = jnp.where(keep, value, 0.0)

    loop(6, update)

    def sent(ref, sem):
        send(ref, ref, sem, own_sem, here).wait_send()

    for n, holds, ref in (
        (0, holds_00, first.at[pl.ds(0, 120), :]),
        (1, holds_00, low.at[pl.ds(0, 15), pl.ds(0, 8), :]),
        (2, holds_10, low.at[pl.ds(0, 15), pl.ds(8, 16), :]),
        (3, holds_11, high.at[pl.ds(0, 15)]),
    ):
        pl.when(holds)(lambda n=n, ref=ref: sent(ref, scatter_send.at[n]))
        pl.when((row == pieces[n][1]) & (core == pieces[n][2]))(lambda n=n, ref=ref: sent(ref, ring_send.at[n]))

    @pl.when(core == 0)
    def _():
        sent(first.at[pl.ds(0, 120), :], plane_send.at[0])
        sent(low.at[pl.ds(0, 15)], plane_send.at[1])
        sent(first, twin_send.at[0])
        sent(low, twin_send.at[1])

    @pl.when(core == 1)
    def _():
        sent(high.at[pl.ds(0, 15)], plane_send.at[2])
        sent(high, twin_send.at[2])

    pl.when(delta < 8)(lambda: sent(top.at[0], top_send.at[0]))
    pl.when((delta == 0) | (delta >= 12))(lambda: sent(top.at[0], top_send.at[1]))
    pl.when((delta >= 2) & (delta <= 8))(lambda: sent(top.at[0], top_send.at[2]))
    pl.when(delta >= 8)(lambda: sent(top.at[0], top_send.at[3]))

    for h in range(2):
        u, v = (x, y) if h == 0 else (y, x)
        p = jnp.where(v == 0, u, v)
        whole = panel.at[core, :, pl.ds(0, 128), :]
        half = panel.at[core, :, pl.ds(0, 64), :]

        @pl.when((v == 0) & (u == 0))
        def _():
            sent(whole, tree_send.at[h, 0])
            sent(whole, tree_send.at[h, 1])

        pl.when((p == 1) | (p == 3))(lambda: sent(half, tree_send.at[h, 2]))

        @pl.when(v == 0)
        def _():
            sent(whole, tree_send.at[h, 3])
            sent(whole, tree_send.at[h, 4])

        sent(whole, pair_send.at[h])


def on_device(slab):
    dma = pltpu.SemaphoreType.DMA
    return pl.pallas_call(
        kernel,
        out_shape=jax.ShapeDtypeStruct(slab.shape, jnp.float32),
        in_specs=[pl.BlockSpec(memory_space=pl.ANY)],
        out_specs=pl.BlockSpec(memory_space=pltpu.VMEM),
        scratch_shapes=[
            pltpu.VMEM((6, NB, NB), jnp.float32),
            pltpu.VMEM((SB, SB), jnp.float32),
            pltpu.VMEM((16, 24, NB), jnp.float32),
            pltpu.VMEM((16, 16, NB), jnp.float32),
            pltpu.VMEM((2, NB, NB), jnp.float32),
            pltpu.VMEM((2, 6, NB, NB), jnp.float32),
            pltpu.VMEM((512, 1024), jnp.float32),
            pltpu.VMEM((SB, SB), jnp.float32),
            dma, dma((4,)), dma((4,)), dma((4,)), dma((4,)), dma((3,)), dma((3,)), dma((3,)), dma((3,)),
            dma((4,)), dma((2, TOP_PARTS)), dma((2, 5)), dma((2, TREE_PARTS, 2)), dma((2,)), dma((2,)),
        ],
        compiler_params=pltpu.CompilerParams(
            collective_id=0, has_side_effects=True, vmem_limit_bytes=60 * 2**20
        ),
    )(slab)


def solution(mesh):
    spec = P(None, "row", "col")
    return jax.shard_map(on_device, mesh=mesh, in_specs=(spec,), out_specs=spec, check_vma=False)
```

time: 1000 us -> 81 us (0.08)
  the two profiles are of different devices: /device:TPU:4 before, /device:TPU:20 now
where the time goes in v2:
time: 81 us; the launch traced here: 80.9 us
  Pallas kernels  78.1 us (96%)
  local copies, waits for them, and re-layouts  2.74 us (3%)
    pallas_call x1, Pallas kernels, on_device(): pl.pallas_call(kernel, out_shape=jax.ShapeDtypeStruct(slab.shape, jnp.flo...  78.1 us
    unnamed x1, local copies, waits for them, and re-layouts  2.74 us

profile of v2, /device:TPU:20, one launch (start us, length us, event | category | flops | bytes accessed | tf_op | source)
XLA Modules:
  0.0 80.9 jit_solution(17846257427057760509)
XLA Ops:
  0.0 78.1 %shard_map.17 = f32[6,256,256]{2,1,0:T(8,128)} custom-call(f32[6,256,256]{2,1,0:T(8,128)} %x_ref.1), custom_call_target="tpu_custom_call" | custom-call | tf_op jit(solution)/shard_map/pallas_call | solution.py:463
  78.1 2.7 %copy.3 = f32[6,256,256]{2,1,0:T(8,128)} copy(f32[6,256,256]{2,1,0:T(8,128)} %shard_map.17) | data formatting | bytes 3145728

commit v3 on v2

v3 whole, which is shorter than its diff:
```python
import jax
import jax.numpy as jnp
from jax import lax
from jax.experimental import pallas as pl
from jax.experimental.pallas import tpu as pltpu
from jax.sharding import PartitionSpec as P

HI = lax.Precision.HIGHEST
SB = 128


def contract(a, b, da, db):
    return lax.dot_general(a, b, (((da,), (db,)), ((), ())), precision=HI, preferred_element_type=jnp.float32)


def dot(a, b):
    return contract(a, b, 1, 0)


def dot_nt(a, b):
    return contract(a, b, 1, 1)


def dot_tn(a, b):
    return contract(a, b, 0, 0)


def lanes(part):
    return jnp.broadcast_to(part, (8, SB))


def eliminate(strips, after):
    sub = lax.broadcasted_iota(jnp.int32, (8, SB), 0)
    lane = lax.broadcasted_iota(jnp.int32, (8, SB), 1)
    strips = list(strips)
    scales = []
    for k in range(16):
        cur = strips[k]
        col = [lanes(cur[:, 8 * k + j:8 * k + j + 1]) for j in range(8)]
        scale = jnp.zeros((8, SB), jnp.float32)
        pairs = []
        for j in range(0, 8, 2):
            a = lanes(col[j][j:j + 1])
            b = lanes(col[j][j + 1:j + 2])
            c = lanes(col[j + 1][j + 1:j + 2])
            det = a * c - b * b
            inv = 1.0 / det
            over_a = 1.0 / a
            scale = jnp.where(sub == j, lax.rsqrt(a), jnp.where(sub == j + 1, lax.rsqrt(det * over_a), scale))
            low0 = jnp.where(sub > j + 1, col[j], 0.0)
            low1 = jnp.where(sub > j + 1, col[j + 1], 0.0)

            def solve(r0, r1):
                return (c * r0 - b * r1) * inv, (a * r1 - b * r0) * inv

            ratios = []
            for i in range(j + 2, 8):
                u, w = solve(lanes(col[i][j:j + 1]), lanes(col[i][j + 1:j + 2]))
                col[i] = col[i] - low0 * u - low1 * w
                ratios.append((u, w))
            r0 = jnp.where(lane == 8 * k + j, a + 1.0, lanes(cur[j:j + 1]))
            r1 = jnp.where(lane == 8 * k + j + 1, c + 1.0, lanes(cur[j + 1:j + 2]))
            u, w = solve(r0, r1)
            cur = cur - low0 * u - low1 * w - jnp.where(sub == j + 1, b * over_a, 0.0) * r0
            pairs.append((ratios, u, w))
        strips[k] = cur
        scales.append(scale)
        for t in range(k + 1, 16):
            acc = strips[t]
            c = [lanes(acc[:, 8 * k + j:8 * k + j + 1]) for j in range(8)]
            for p, (ratios, u, w) in enumerate(pairs):
                c0, c1 = c[2 * p], c[2 * p + 1]
                for i, (ui, wi) in enumerate(ratios):
                    c[2 * p + 2 + i] = c[2 * p + 2 + i] - c0 * ui - c1 * wi
                acc = acc - c0 * u - c1 * w
            strips[t] = acc
        after(k)
    return strips, scales


def block(i):
    return pl.ds(pl.multiple_of(i * SB, SB), SB)


def factor(a, m, z, lb, xs, hook, unpack):
    sub = lax.broadcasted_iota(jnp.int32, (8, SB), 0)
    lane = lax.broadcasted_iota(jnp.int32, (8, SB), 1)
    xs[...] = jnp.zeros((SB, SB), jnp.float32)
    lb[...] = jnp.zeros((3, SB, SB), jnp.float32)

    def step(s, carry):
        p = jnp.maximum(s - 1, 0)

        def lower(i):
            lb[i] = dot_nt(a[block(s + i), block(p)], xs[...])

        def schur(i, j):
            a[block(s + i), block(s + j)] = a[block(s + i), block(s + j)] - dot_nt(lb[i], lb[j])

        def rows():
            z[block(p), :] = dot(xs[...], m[block(p), :])

        def spread(i):
            m[block(s + i), :] = m[block(s + i), :] - dot(lb[i], z[block(p), :])

        jobs = {
            0: (lambda: lower(1), lambda: lower(2)),
            1: (rows,),
            3: (lambda: schur(1, 0), lambda: schur(1, 1)),
            4: (lambda: schur(2, 0), lambda: schur(2, 1)),
            5: (lambda: schur(2, 2),),
            6: (lambda: spread(0),),
            9: (lambda: spread(1),),
            12: (lambda: spread(2),),
        }

        def after(k):
            for job in jobs.get(k, ()):
                job()
            hook(s, k)

        strips, scales = eliminate([a[pl.ds(pl.multiple_of(s * SB + 8 * t, 8), 8), block(s)] for t in range(16)], after)
        unpack(s)
        for t in range(16):
            diag = sub + 8 * t
            xs[8 * t:8 * t + 8, :] = jnp.where(
                lane < diag, strips[t] * scales[t], jnp.where(lane == diag, scales[t], 0.0))
        lb[0] = dot_nt(a[block(s + 1), block(s)], xs[...])
        a[block(s + 1), block(s + 1)] = a[block(s + 1), block(s + 1)] - dot_nt(lb[0], lb[0])
        return carry

    lax.fori_loop(0, 4, step, 0)
    z[block(3), :] = dot(xs[...], m[block(3), :])

NB = 256
N_ROW = 16
N_COL = 32
MESH = pl.DeviceIdType.MESH
TREE_PARTS = 12
TOP_PARTS = 8
SKEW = 5
EARLY = 10
VMEM = 28 * 2**20


def halves(v):
    hi = v.astype(jnp.bfloat16)
    return hi, (v - hi.astype(jnp.float32)).astype(jnp.bfloat16)


def dot16(p, q):
    return lax.dot_general(p, q, (((1,), (0,)), ((), ())), preferred_element_type=jnp.float32)


def send(src, dst, send_sem, recv_sem, device):
    return pltpu.make_async_remote_copy(
        src_ref=src, dst_ref=dst, send_sem=send_sem, recv_sem=recv_sem, device_id=device, device_id_type=MESH
    )


def kernel(
    x_ref, o_ref, own, first, low, high, top, panel, a, m, z, lb, xs, w_hi, w_lo,
    own_sem, scatter_send, scatter_recv, ring_send, ring_recv, plane_send, plane_recv, twin_send, twin_recv,
    top_send, top_recv, tree_send, tree_recv, pair_send, pair_recv,
):
    row = lax.axis_index("row")
    col = lax.axis_index("col")
    core = lax.rem(col, 2)
    chip = col // 2
    x = chip // 4
    y = lax.rem(chip, 4)
    is_root = col < 2
    twin = (row, col + 1 - 2 * core)
    here = (row, col)

    own_copy = pltpu.make_async_copy(x_ref, own, own_sem)
    own_copy.start()

    def loop(n, body):
        def one(i, carry):
            body(i)
            return carry
        lax.fori_loop(0, n, one, 0)

    def plane_peer(j):
        o = 10 + j
        o = jnp.where(o >= 16, o - 15, o)
        return lax.rem(x + o // 4, 4) * 4 + lax.rem(y + lax.rem(o, 4), 4)

    def ring_peer(j):
        half = (j + 1) // 2
        return lax.rem(row + 8 + jnp.where(lax.rem(j, 2) == 1, -half, half) + N_ROW, N_ROW)

    barrier = pltpu.get_barrier_semaphore()
    loop(15, lambda j: pl.semaphore_signal(barrier, inc=1, device_id=(ring_peer(j), col), device_id_type=MESH))
    loop(15, lambda j: pl.semaphore_signal(
        barrier, inc=1, device_id=(row, plane_peer(j) * 2 + core), device_id_type=MESH))
    pl.semaphore_signal(barrier, inc=1, device_id=twin, device_id_type=MESH)
    wide_r = lax.broadcasted_iota(jnp.int32, (768, 512), 0)
    wide_c = lax.broadcasted_iota(jnp.int32, (768, 512), 1)
    m[...] = jnp.where(wide_r == wide_c, 1.0, 0.0)
    a[...] = jnp.zeros((768, 768), jnp.float32)
    own_copy.wait()

    def first_piece(i):
        return first.at[pl.ds(pl.multiple_of(i * 8, 8), 8), :]

    holds_00 = (row == 0) & (col == 0)
    holds_10 = (row == 1) & (col == 0)
    holds_11 = (row == 1) & (col == 1)

    @pl.when(holds_00)
    def _():
        first[0:8, :] = own[0, 0:8, 0:SB]
        low[0, 0:8, :] = own[0, SB:SB + 8, :]

    @pl.when(holds_10)
    def _():
        low[0, 8:24, :] = own[0, 0:16, :]

    @pl.when(holds_11)
    def _():
        high[0] = own[0, 0:16, :]

    @pl.when(is_root)
    def _():
        panel[core] = own[...]

    @pl.when(row < 2)
    def _():
        top[row] = own[0]

    pl.semaphore_wait(barrier, 31)

    def own_rows(start, n):
        return own.at[0, pl.ds(pl.multiple_of(start, 8), n), :]

    @pl.when(holds_00)
    def _():
        loop(15, lambda j: send(
            own.at[0, pl.ds(pl.multiple_of(plane_peer(j) * 8, 8), 8), pl.ds(0, SB)], first_piece(plane_peer(j)),
            scatter_send.at[0], scatter_recv.at[0], (row, plane_peer(j) * 2)).start())
        loop(15, lambda j: send(
            own_rows(SB + plane_peer(j) * 8, 8), low.at[plane_peer(j), pl.ds(0, 8), :],
            scatter_send.at[1], scatter_recv.at[1], (row, plane_peer(j) * 2)).start())

    @pl.when(holds_10)
    def _():
        loop(15, lambda j: send(
            own_rows(plane_peer(j) * 16, 16), low.at[plane_peer(j), pl.ds(8, 16), :],
            scatter_send.at[2], scatter_recv.at[2], (row, plane_peer(j) * 2)).start())

    @pl.when(holds_11)
    def _():
        loop(15, lambda j: send(
            own_rows(plane_peer(j) * 16, 16), high.at[plane_peer(j)],
            scatter_send.at[3], scatter_recv.at[3], (row, plane_peer(j) * 2 + 1)).start())

    q = lax.rem(row, 2)
    delta = row - q
    top_depth = jnp.where(delta <= 8, delta, N_ROW - delta) // 2

    def top_to(offset):
        return (lax.rem(row + offset + N_ROW, N_ROW), col)

    def top_step(t):
        m = t - SKEW * top_depth
        slot = jnp.clip(m, 0, TOP_PARTS - 1)
        piece = top.at[q, pl.ds(pl.multiple_of(slot * 32, 32), 32), :]

        def go(kind, offset):
            send(piece, piece, top_send.at[kind], top_recv.at[q, slot], top_to(offset)).start()

        @pl.when((m >= 0) & (m < TOP_PARTS))
        def _():
            @pl.when(delta > 0)
            def _():
                send(piece, piece, top_send.at[0], top_recv.at[q, slot], here).wait_recv()

            @pl.when(delta < 8)
            def _():
                go(0, 2)

            @pl.when((delta == 0) | (delta >= 12))
            def _():
                go(1, -2)

            @pl.when((delta >= 2) & (delta <= 8))
            def _():
                go(2, -1)

            @pl.when(delta >= 8)
            def _():
                go(3, 1)

    def hops(p):
        return jnp.where(p == 0, 0, jnp.where(p == 2, 2, 1))

    def tree_step(t):
        for h in range(2):
            u, v = (x, y) if h == 0 else (y, x)
            p = jnp.where(v == 0, u, v)
            late = (u == 0) & (v != 0)

            def at(u2, v2):
                x2, y2 = (u2, v2) if h == 0 else (v2, u2)
                return (row, x2 * 8 + y2 * 2 + core)

            m = t - SKEW * (jnp.where(late, 2, hops(u)) + hops(v))
            slot = jnp.clip(m, 0, TREE_PARTS - 1)
            start = 128 * h + 64 * lax.rem(slot, 2)
            part = panel.at[core, slot // 2, pl.ds(pl.multiple_of(start, 64), 64), :]
            half0 = panel.at[core, slot // 2, pl.ds(pl.multiple_of(start, 32), 32), :]
            half1 = panel.at[core, slot // 2, pl.ds(pl.multiple_of(start + 32, 32), 32), :]

            def go(piece, kind, half, device):
                send(piece, piece, tree_send.at[h, kind], tree_recv.at[h, slot, half], device).start()

            @pl.when((m >= 0) & (m < TREE_PARTS))
            def _():
                @pl.when(((p == 1) | (p == 3)) & jnp.logical_not(late))
                def _():
                    send(part, part, tree_send.at[h, 0], tree_recv.at[h, slot, 0], here).wait_recv()

                @pl.when((p == 2) | late)
                def _():
                    send(half0, half0, tree_send.at[h, 0], tree_recv.at[h, slot, 0], here).wait_recv()
                    send(half1, half1, tree_send.at[h, 0], tree_recv.at[h, slot, 1], here).wait_recv()

                @pl.when((v == 0) & (u == 0))
                def _():
                    go(part, 0, 0, at(1, 0))
                    go(part, 1, 0, at(3, 0))

                @pl.when((p == 1) & jnp.logical_not(late))
                def _():
                    go(half0, 2, 0, at(jnp.where(v == 0, 2, u), jnp.where(v == 0, 0, 2)))

                @pl.when((p == 3) & jnp.logical_not(late))
                def _():
                    go(half1, 2, 1, at(jnp.where(v == 0, 2, u), jnp.where(v == 0, 0, 2)))

                @pl.when((v == 0) & (u != 0))
                def _():
                    go(part, 3, 0, at(u, 1))
                    go(part, 4, 0, at(u, 3))

                @pl.when((v != 0) & (u == 1))
                def _():
                    go(half0, 5, 0, at(0, v))

                @pl.when((v != 0) & (u == 3))
                def _():
                    go(half1, 5, 1, at(0, v))

                send(part, part, pair_send.at[h], pair_recv.at[h], twin).start()

    def tick(t):
        top_step(t)
        tree_step(t)

    def ticks(start, stop):
        def one(t, carry):
            tick(t)
            return carry
        lax.fori_loop(start, stop, one, 0)

    pieces = (
        (first_piece(chip), 0, 0),
        (low.at[chip, pl.ds(0, 8), :], 0, 0),
        (low.at[chip, pl.ds(8, 16), :], 1, 0),
        (high.at[chip], 1, 1),
    )
    def scattered(n):
        piece, start, carrier = pieces[n]

        @pl.when((row == start) & (core == carrier) & (chip != 0))
        def _():
            send(piece, piece, scatter_send.at[n], scatter_recv.at[n], here).wait_recv()

    def along_ring(n):
        piece, start, carrier = pieces[n]

        @pl.when((row == start) & (core == carrier))
        def _():
            loop(15, lambda j: send(piece, piece, ring_send.at[n], ring_recv.at[n], (ring_peer(j), col)).start())

    def ring_arrived(n):
        piece, start, _ = pieces[n]

        @pl.when(row != start)
        def _():
            send(piece, piece, ring_send.at[n], ring_recv.at[n], here).wait_recv()

    scattered(0)

    @pl.when(core == 0)
    def _():
        ring_arrived(0)
        loop(15, lambda j: send(
            first_piece(chip), first_piece(chip), plane_send.at[0], plane_recv.at[0],
            (row, plane_peer(j) * 2)).start())

    along_ring(0)
    for n in range(1, 4):
        scattered(n)
        along_ring(n)
    ticks(0, 6)

    @pl.when(core == 0)
    def _():
        ring_arrived(1)
        ring_arrived(2)
        loop(15, lambda j: send(
            low.at[chip], low.at[chip], plane_send.at[1], plane_recv.at[1], (row, plane_peer(j) * 2)).start())

    @pl.when(core == 1)
    def _():
        ring_arrived(3)
        loop(15, lambda j: send(
            high.at[chip], high.at[chip], plane_send.at[2], plane_recv.at[2],
            (row, plane_peer(j) * 2 + 1)).start())

    ticks(6, EARLY)

    @pl.when(core == 0)
    def _():
        send(first.at[pl.ds(0, 120), :], first.at[pl.ds(0, 120), :], plane_send.at[0], plane_recv.at[0], here).wait_recv()
        send(first, first, twin_send.at[0], twin_recv.at[0], twin).start()

    @pl.when(core == 1)
    def _():
        send(first, first, twin_send.at[0], twin_recv.at[0], here).wait_recv()

    def rest_in_plane():
        @pl.when(core == 0)
        def _():
            send(low.at[pl.ds(0, 15)], low.at[pl.ds(0, 15)], plane_send.at[1], plane_recv.at[1], here).wait_recv()
            send(low, low, twin_send.at[1], twin_recv.at[1], twin).start()

        @pl.when(core == 1)
        def _():
            send(high.at[pl.ds(0, 15)], high.at[pl.ds(0, 15)], plane_send.at[2], plane_recv.at[2], here).wait_recv()
            send(high, high, twin_send.at[2], twin_recv.at[2], twin).start()

    def rest_from_twin():
        @pl.when(core == 1)
        def _():
            send(low, low, twin_send.at[1], twin_recv.at[1], here).wait_recv()

        @pl.when(core == 0)
        def _():
            send(high, high, twin_send.at[2], twin_recv.at[2], here).wait_recv()

        for i in range(16):
            a[SB + 8 * i:SB + 8 * i + 8, 0:NB] = low[i, 0:8, :]
            a[NB + 16 * i:NB + 16 * i + 16, 0:NB] = low[i, 8:24, :]
            a[NB + 16 * i:NB + 16 * i + 16, NB:2 * NB] = high[i]

    a[0:SB, 0:SB] = first[...]

    def hook(s, k):
        if k % 3 == 2:
            if k == 8:
                pl.when(s == 0)(rest_in_plane)
            tick(EARLY + 6 * s + k // 3)

    def unpack(s):
        pl.when(s == 0)(rest_from_twin)
        tick(EARLY + 6 * s + 5)

    factor(a, m, z, lb, xs, hook, unpack)

    def top_arrived(m):
        piece = top.at[1 - q, pl.ds(pl.multiple_of(m * 32, 32), 32), :]
        send(piece, piece, top_send.at[0], top_recv.at[1 - q, m], here).wait_recv()

    @pl.when((row != 0) | (q != 1))
    def _():
        loop(TOP_PARTS, top_arrived)

    sq_r = lax.broadcasted_iota(jnp.int32, (NB, NB), 0)
    sq_c = lax.broadcasted_iota(jnp.int32, (NB, NB), 1)
    pick = jnp.where(sq_r == sq_c, -1.0, 0.0)
    upper = dot(z[0:NB, 0:NB], top[0])
    under = dot(z[NB:2 * NB, 0:NB], top[0]) + dot(z[NB:2 * NB, NB:2 * NB], top[1])
    upper = jnp.where(is_root, jnp.where(col == 0, pick, 0.0), upper)
    under = jnp.where(is_root, jnp.where(col == 1, pick, 0.0), under)
    w_hi[0:NB], w_lo[0:NB] = halves(dot_tn(z[0:NB, 0:NB], upper) + dot_tn(z[NB:2 * NB, 0:NB], under))
    w_hi[NB:2 * NB], w_lo[NB:2 * NB] = halves(dot_tn(z[NB:2 * NB, NB:2 * NB], under))

    for h in range(2):
        part = panel.at[1 - core, :, pl.ds(128 * h, 128), :]
        send(part, part, pair_send.at[h], pair_recv.at[h], here).wait_recv()

    for g in range(6):
        index = g * N_ROW + row
        value = jnp.where(is_root, 0.0, own[g])
        for k in range(2):
            hi, lo = halves(panel[k, g])
            w1, w2 = w_hi[NB * k:NB * k + NB], w_lo[NB * k:NB * k + NB]
            value = value - (dot16(hi, w1) + (dot16(hi, w2) + dot16(lo, w1)))
        keep = (index > col) | ((index == col) & ((sq_r >= sq_c) | jnp.logical_not(is_root)))
        o_ref[g] = jnp.where(keep, value, 0.0)

    def sent(ref, sem):
        send(ref, ref, sem, own_sem, here).wait_send()

    for n, holds, ref in (
        (0, holds_00, first.at[pl.ds(0, 120), :]),
        (1, holds_00, low.at[pl.ds(0, 15), pl.ds(0, 8), :]),
        (2, holds_10, low.at[pl.ds(0, 15), pl.ds(8, 16), :]),
        (3, holds_11, high.at[pl.ds(0, 15)]),
    ):
        pl.when(holds)(lambda n=n, ref=ref: sent(ref, scatter_send.at[n]))
        pl.when((row == pieces[n][1]) & (core == pieces[n][2]))(lambda n=n, ref=ref: sent(ref, ring_send.at[n]))

    @pl.when(core == 0)
    def _():
        sent(first.at[pl.ds(0, 120), :], plane_send.at[0])
        sent(low.at[pl.ds(0, 15)], plane_send.at[1])
        sent(first, twin_send.at[0])
        sent(low, twin_send.at[1])

    @pl.when(core == 1)
    def _():
        sent(high.at[pl.ds(0, 15)], plane_send.at[2])
        sent(high, twin_send.at[2])

    pl.when(delta < 8)(lambda: sent(top.at[0], top_send.at[0]))
    pl.when((delta == 0) | (delta >= 12))(lambda: sent(top.at[0], top_send.at[1]))
    pl.when((delta >= 2) & (delta <= 8))(lambda: sent(top.at[0], top_send.at[2]))
    pl.when(delta >= 8)(lambda: sent(top.at[0], top_send.at[3]))

    for h in range(2):
        u, v = (x, y) if h == 0 else (y, x)
        p = jnp.where(v == 0, u, v)
        whole = panel.at[core, :, pl.ds(0, 128), :]
        half = panel.at[core, :, pl.ds(0, 64), :]

        @pl.when((v == 0) & (u == 0))
        def _():
            sent(whole, tree_send.at[h, 0])
            sent(whole, tree_send.at[h, 1])

        pl.when(((p == 1) | (p == 3)) & ((v == 0) | (u != 0)))(lambda: sent(half, tree_send.at[h, 2]))
        pl.when((v != 0) & ((u == 1) | (u == 3)))(lambda: sent(half, tree_send.at[h, 5]))

        @pl.when((v == 0) & (u != 0))
        def _():
            sent(whole, tree_send.at[h, 3])
            sent(whole, tree_send.at[h, 4])

        sent(whole, pair_send.at[h])


def on_device(slab):
    dma = pltpu.SemaphoreType.DMA
    return pl.pallas_call(
        kernel,
        out_shape=jax.ShapeDtypeStruct(slab.shape, jnp.float32),
        in_specs=[pl.BlockSpec(memory_space=pl.ANY)],
        out_specs=pl.BlockSpec(memory_space=pltpu.VMEM),
        scratch_shapes=[
            pltpu.VMEM((6, NB, NB), jnp.float32),
            pltpu.VMEM((SB, SB), jnp.float32),
            pltpu.VMEM((16, 24, NB), jnp.float32),
            pltpu.VMEM((16, 16, NB), jnp.float32),
            pltpu.VMEM((2, NB, NB), jnp.float32),
            pltpu.VMEM((2, 6, NB, NB), jnp.float32),
            pltpu.VMEM((768, 768), jnp.float32),
            pltpu.VMEM((768, 512), jnp.float32),
            pltpu.VMEM((512, 512), jnp.float32),
            pltpu.VMEM((3, SB, SB), jnp.float32),
            pltpu.VMEM((SB, SB), jnp.float32),
            pltpu.VMEM((512, NB), jnp.bfloat16),
            pltpu.VMEM((512, NB), jnp.bfloat16),
            dma, dma((4,)), dma((4,)), dma((4,)), dma((4,)), dma((3,)), dma((3,)), dma((3,)), dma((3,)),
            dma((4,)), dma((2, TOP_PARTS)), dma((2, 6)), dma((2, TREE_PARTS, 2)), dma((2,)), dma((2,)),
        ],
        compiler_params=pltpu.CompilerParams(
            collective_id=0, has_side_effects=True, vmem_limit_bytes=VMEM
        ),
    )(slab)


def solution(mesh):
    spec = P(None, "row", "col")
    return jax.shard_map(on_device, mesh=mesh, in_specs=(spec,), out_specs=spec, check_vma=False)
```

time: 81 us -> 62.8 us (0.78)
  the two profiles are of different devices: /device:TPU:20 before, /device:TPU:98 now
where the time goes in v3:
time: 62.8 us; the launch traced here: 62.7 us
  Pallas kernels  60.1 us (96%)
  local copies, waits for them, and re-layouts  2.55 us (4%)
    pallas_call x1, Pallas kernels, on_device(): pl.pallas_call(kernel, out_shape=jax.ShapeDtypeStruct(slab.shape, jnp.flo...  60.1 us
    unnamed x3, local copies, waits for them, and re-layouts  2.55 us

profile of v3, /device:TPU:98, one launch (start us, length us, event | category | flops | bytes accessed | tf_op | source)
XLA Modules:
  0.0 62.7 jit_solution(10796107776724097385)
XLA Ops:
  0.0 0.0 copy-start
  0.0 1.4 %copy-done = f32[6,256,256]{2,1,0:T(8,128)S(1)} copy-done((f32[6,256,256]{2,1,0:T(8,128)S(1)}, f32[6,256,256]{2,1,0:T(8,128)}, u32[]{:S(2)}) %copy-start) | copy-done | bytes 1572888
  1.4 60.1 %shard_map.17 = f32[6,256,256]{2,1,0:T(8,128)S(1)} custom-call(f32[6,256,256]{2,1,0:T(8,128)S(1)} %copy-done), custom_call_target="tpu_custom_call" | custom-call | tf_op jit(solution)/shard_map/pallas_call | solution.py:559
  61.6 1.1 %copy.3 = f32[6,256,256]{2,1,0:T(8,128)} copy(f32[6,256,256]{2,1,0:T(8,128)S(1)} %shard_map.17) | data formatting | bytes 3145728
Async XLA Ops:
  0.0 1.4 %copy-start = (f32[6,256,256]{2,1,0:T(8,128)S(1)}, f32[6,256,256]{2,1,0:T(8,128)}, u32[]{:S(2)}) copy-start(f32[6,256,256]{2,1,0:T(8,128)} %x_ref.1) | copy-start | bytes 4718596

commit v4 on v3

--- a/solution.py
+++ b/solution.py
@@ -125,8 +125,11 @@
             diag = sub + 8 * t
             xs[8 * t:8 * t + 8, :] = jnp.where(
                 lane < diag, strips[t] * scales[t], jnp.where(lane == diag, scales[t], 0.0))
-        lb[0] = dot_nt(a[block(s + 1), block(s)], xs[...])
-        a[block(s + 1), block(s + 1)] = a[block(s + 1), block(s + 1)] - dot_nt(lb[0], lb[0])
+
+        @pl.when(s < 3)
+        def _():
+            lb[0] = dot_nt(a[block(s + 1), block(s)], xs[...])
+            a[block(s + 1), block(s + 1)] = a[block(s + 1), block(s + 1)] - dot_nt(lb[0], lb[0])
         return carry
 
     lax.fori_loop(0, 4, step, 0)
@@ -136,10 +139,17 @@
 N_ROW = 16
 N_COL = 32
 MESH = pl.DeviceIdType.MESH
-TREE_PARTS = 12
-TOP_PARTS = 8
-SKEW = 5
-EARLY = 10
+TREE_PARTS = 6
+TOP_PARTS = 4
+SKEW = 3
+TOP_LAG = 2
+FAR_TICKS = 3
+NEAR_TICKS = 3
+MID_TICKS = 4
+EARLY = 6
+TICKS = (4, 9, 14)
+TREE_ROWS = 768 // TREE_PARTS
+TOP_ROWS = NB // TOP_PARTS
 VMEM = 28 * 2**20
 
 
@@ -260,13 +270,20 @@
     delta = row - q
     top_depth = jnp.where(delta <= 8, delta, N_ROW - delta) // 2
 
+    top_goes = (
+        delta < 8,
+        (delta == 0) | (delta >= 12),
+        (delta >= 2) & (delta <= 8),
+        delta >= 8,
+    )
+
     def top_to(offset):
         return (lax.rem(row + offset + N_ROW, N_ROW), col)
 
     def top_step(t):
-        m = t - SKEW * top_depth
+        m = t - jnp.where(delta == 0, 0, TOP_LAG + SKEW * top_depth)
         slot = jnp.clip(m, 0, TOP_PARTS - 1)
-        piece = top.at[q, pl.ds(pl.multiple_of(slot * 32, 32), 32), :]
+        piece = top.at[q, pl.ds(pl.multiple_of(slot * TOP_ROWS, TOP_ROWS), TOP_ROWS), :]
 
         def go(kind, offset):
             send(piece, piece, top_send.at[kind], top_recv.at[q, slot], top_to(offset)).start()
@@ -277,21 +294,8 @@
             def _():
                 send(piece, piece, top_send.at[0], top_recv.at[q, slot], here).wait_recv()
 
-            @pl.when(delta < 8)
-            def _():
-                go(0, 2)
-
-            @pl.when((delta == 0) | (delta >= 12))
-            def _():
-                go(1, -2)
-
-            @pl.when((delta >= 2) & (delta <= 8))
-            def _():
-                go(2, -1)
-
-            @pl.when(delta >= 8)
-            def _():
-                go(3, 1)
+            for kind, offset in enumerate((2, -2, -1, 1)):
+                pl.when(top_goes[kind])(lambda kind=kind, offset=offset: go(kind, offset))
 
     def hops(p):
         return jnp.where(p == 0, 0, jnp.where(p == 2, 2, 1))
@@ -308,10 +312,10 @@
 
             m = t - SKEW * (jnp.where(late, 2, hops(u)) + hops(v))
             slot = jnp.clip(m, 0, TREE_PARTS - 1)
-            start = 128 * h + 64 * lax.rem(slot, 2)
-            part = panel.at[core, slot // 2, pl.ds(pl.multiple_of(start, 64), 64), :]
-            half0 = panel.at[core, slot // 2, pl.ds(pl.multiple_of(start, 32), 32), :]
-            half1 = panel.at[core, slot // 2, pl.ds(pl.multiple_of(start + 32, 32), 32), :]
+            start = 128 * h + TREE_ROWS * lax.rem(slot, TREE_PARTS // 6)
+            part = panel.at[core, slot // (TREE_PARTS // 6), pl.ds(pl.multiple_of(start, TREE_ROWS), TREE_ROWS), :]
+            half0 = panel.at[core, slot // (TREE_PARTS // 6), pl.ds(pl.multiple_of(start, TREE_ROWS // 2), TREE_ROWS // 2), :]
+            half1 = panel.at[core, slot // (TREE_PARTS // 6), pl.ds(pl.multiple_of(start + TREE_ROWS // 2, TREE_ROWS // 2), TREE_ROWS // 2), :]
 
             def go(piece, kind, half, device):
                 send(piece, piece, tree_send.at[h, kind], tree_recv.at[h, slot, half], device).start()
@@ -392,20 +396,27 @@
         def _():
             send(piece, piece, ring_send.at[n], ring_recv.at[n], here).wait_recv()
 
-    scattered(0)
-
-    @pl.when(core == 0)
-    def _():
-        ring_arrived(0)
+    def gather_first():
         loop(15, lambda j: send(
             first_piece(chip), first_piece(chip), plane_send.at[0], plane_recv.at[0],
             (row, plane_peer(j) * 2)).start())
 
-    along_ring(0)
-    for n in range(1, 4):
-        scattered(n)
+    pl.when(row >= 2)(lambda: ticks(0, FAR_TICKS))
+    scattered(0)
+    pl.when((row == 0) & (core == 0))(gather_first)
+    for n in range(4):
+        if n:
+            scattered(n)
         along_ring(n)
-    ticks(0, 6)
+    pl.when(row < 2)(lambda: ticks(0, NEAR_TICKS))
+
+    @pl.when((row != 0) & (core == 0))
+    def _():
+        ring_arrived(0)
+        gather_first()
+
+    pl.when(row < 2)(lambda: ticks(NEAR_TICKS, FAR_TICKS))
+    ticks(FAR_TICKS, MID_TICKS)
 
     @pl.when(core == 0)
     def _():
@@ -421,7 +432,7 @@
             high.at[chip], high.at[chip], plane_send.at[2], plane_recv.at[2],
             (row, plane_peer(j) * 2 + 1)).start())
 
-    ticks(6, EARLY)
+    ticks(MID_TICKS, EARLY)
 
     @pl.when(core == 0)
     def _():
@@ -460,19 +471,18 @@
     a[0:SB, 0:SB] = first[...]
 
     def hook(s, k):
-        if k % 3 == 2:
-            if k == 8:
-                pl.when(s == 0)(rest_in_plane)
-            tick(EARLY + 6 * s + k // 3)
+        if k == 7:
+            pl.when(s == 0)(rest_in_plane)
+        if k in TICKS:
+            tick(EARLY + len(TICKS) * s + TICKS.index(k))
 
     def unpack(s):
         pl.when(s == 0)(rest_from_twin)
-        tick(EARLY + 6 * s + 5)
 
     factor(a, m, z, lb, xs, hook, unpack)
 
     def top_arrived(m):
-        piece = top.at[1 - q, pl.ds(pl.multiple_of(m * 32, 32), 32), :]
+        piece = top.at[1 - q, pl.ds(pl.multiple_of(m * TOP_ROWS, TOP_ROWS), TOP_ROWS), :]
         send(piece, piece, top_send.at[0], top_recv.at[1 - q, m], here).wait_recv()
 
     @pl.when((row != 0) | (q != 1))
@@ -527,10 +537,8 @@
         sent(high.at[pl.ds(0, 15)], plane_send.at[2])
         sent(high, twin_send.at[2])
 
-    pl.when(delta < 8)(lambda: sent(top.at[0], top_send.at[0]))
-    pl.when((delta == 0) | (delta >= 12))(lambda: sent(top.at[0], top_send.at[1]))
-    pl.when((delta >= 2) & (delta <= 8))(lambda: sent(top.at[0], top_send.at[2]))
-    pl.when(delta >= 8)(lambda: sent(top.at[0], top_send.at[3]))
+    for kind in range(4):
+        pl.when(top_goes[kind])(lambda kind=kind: sent(top.at[0], top_send.at[kind]))
 
     for h in range(2):
         u, v = (x, y) if h == 0 else (y, x)

time: 62.8 us -> 61.1 us (0.973)
  the two profiles are of different devices: /device:TPU:98 before, /device:TPU:234 now
where the time goes in v4:
time: 61.1 us; the launch traced here: 60.9 us
  Pallas kernels  58.4 us (96%)
  local copies, waits for them, and re-layouts  2.55 us (4%)
    pallas_call x1, Pallas kernels, on_device(): pl.pallas_call(kernel, out_shape=jax.ShapeDtypeStruct(slab.shape, jnp.flo...  58.4 us
    unnamed x3, local copies, waits for them, and re-layouts  2.55 us

profile of v4, /device:TPU:234, one launch (start us, length us, event | category | flops | bytes accessed | tf_op | source)
XLA Modules:
  0.0 60.9 jit_solution(17391517811249270006)
XLA Ops:
  0.0 0.0 copy-start
  0.0 1.4 %copy-done = f32[6,256,256]{2,1,0:T(8,128)S(1)} copy-done((f32[6,256,256]{2,1,0:T(8,128)S(1)}, f32[6,256,256]{2,1,0:T(8,128)}, u32[]{:S(2)}) %copy-start) | copy-done | bytes 1572888
  1.4 58.4 %shard_map.17 = f32[6,256,256]{2,1,0:T(8,128)S(1)} custom-call(f32[6,256,256]{2,1,0:T(8,128)S(1)} %copy-done), custom_call_target="tpu_custom_call" | custom-call | tf_op jit(solution)/shard_map/pallas_call | solution.py:567
  59.8 1.1 %copy.3 = f32[6,256,256]{2,1,0:T(8,128)} copy(f32[6,256,256]{2,1,0:T(8,128)S(1)} %shard_map.17) | data formatting | bytes 3145728
Async XLA Ops:
  0.0 1.4 %copy-start = (f32[6,256,256]{2,1,0:T(8,128)S(1)}, f32[6,256,256]{2,1,0:T(8,128)}, u32[]{:S(2)}) copy-start(f32[6,256,256]{2,1,0:T(8,128)} %x_ref.1) | copy-start | bytes 4718596

commit v5 on v4

--- a/solution.py
+++ b/solution.py
@@ -162,6 +162,15 @@
     return lax.dot_general(p, q, (((1,), (0,)), ((), ())), preferred_element_type=jnp.float32)
 
 
+def dot3(p, q, dim):
+    (p1, p2), (q1, q2) = halves(p), halves(q)
+
+    def one(u, v):
+        return lax.dot_general(u, v, (((dim,), (0,)), ((), ())), preferred_element_type=jnp.float32)
+
+    return one(p1, q1) + (one(p1, q2) + one(p2, q1))
+
+
 def send(src, dst, send_sem, recv_sem, device):
     return pltpu.make_async_remote_copy(
         src_ref=src, dst_ref=dst, send_sem=send_sem, recv_sem=recv_sem, device_id=device, device_id_type=MESH
@@ -492,12 +501,12 @@
     sq_r = lax.broadcasted_iota(jnp.int32, (NB, NB), 0)
     sq_c = lax.broadcasted_iota(jnp.int32, (NB, NB), 1)
     pick = jnp.where(sq_r == sq_c, -1.0, 0.0)
-    upper = dot(z[0:NB, 0:NB], top[0])
-    under = dot(z[NB:2 * NB, 0:NB], top[0]) + dot(z[NB:2 * NB, NB:2 * NB], top[1])
+    upper = dot3(z[0:NB, 0:NB], top[0], 1)
+    under = dot3(z[NB:2 * NB, 0:NB], top[0], 1) + dot3(z[NB:2 * NB, NB:2 * NB], top[1], 1)
     upper = jnp.where(is_root, jnp.where(col == 0, pick, 0.0), upper)
     under = jnp.where(is_root, jnp.where(col == 1, pick, 0.0), under)
-    w_hi[0:NB], w_lo[0:NB] = halves(dot_tn(z[0:NB, 0:NB], upper) + dot_tn(z[NB:2 * NB, 0:NB], under))
-    w_hi[NB:2 * NB], w_lo[NB:2 * NB] = halves(dot_tn(z[NB:2 * NB, NB:2 * NB], under))
+    w_hi[0:NB], w_lo[0:NB] = halves(dot3(z[0:NB, 0:NB], upper, 0) + dot3(z[NB:2 * NB, 0:NB], under, 0))
+    w_hi[NB:2 * NB], w_lo[NB:2 * NB] = halves(dot3(z[NB:2 * NB, NB:2 * NB], under, 0))
 
     for h in range(2):
         part = panel.at[1 - core, :, pl.ds(128 * h, 128), :]

time: 61.1 us -> 60 us (0.982)
  Pallas kernels: 58.4 us -> 57.3 us
    pallas_call x1, Pallas kernels: 58.4 us -> 57.3 us  [on_device(): pl.pallas_call(kernel, out_shape=jax.ShapeDtypeStruct(slab.shape, jnp.flo...]
where the time goes in v5:
time: 60 us; the launch traced here: 59.9 us
  Pallas kernels  57.3 us (96%)
  local copies, waits for them, and re-layouts  2.55 us (4%)
    pallas_call x1, Pallas kernels, on_device(): pl.pallas_call(kernel, out_shape=jax.ShapeDtypeStruct(slab.shape, jnp.flo...  57.3 us
    unnamed x3, local copies, waits for them, and re-layouts  2.55 us

profile of v5, /device:TPU:234, one launch (start us, length us, event | category | flops | bytes accessed | tf_op | source)
XLA Modules:
  0.0 59.9 jit_solution(4410857327940487524)
XLA Ops:
  0.0 0.0 copy-start
  0.0 1.4 %copy-done = f32[6,256,256]{2,1,0:T(8,128)S(1)} copy-done((f32[6,256,256]{2,1,0:T(8,128)S(1)}, f32[6,256,256]{2,1,0:T(8,128)}, u32[]{:S(2)}) %copy-start) | copy-done | bytes 1572888
  1.4 57.3 %shard_map.17 = f32[6,256,256]{2,1,0:T(8,128)S(1)} custom-call(f32[6,256,256]{2,1,0:T(8,128)S(1)} %copy-done), custom_call_target="tpu_custom_call" | custom-call | tf_op jit(solution)/shard_map/pallas_call | solution.py:576
  58.8 1.1 %copy.3 = f32[6,256,256]{2,1,0:T(8,128)} copy(f32[6,256,256]{2,1,0:T(8,128)S(1)} %shard_map.17) | data formatting | bytes 3145728
Async XLA Ops:
  0.0 1.4 %copy-start = (f32[6,256,256]{2,1,0:T(8,128)S(1)}, f32[6,256,256]{2,1,0:T(8,128)}, u32[]{:S(2)}) copy-start(f32[6,256,256]{2,1,0:T(8,128)} %x_ref.1) | copy-start | bytes 4718596
